TPU v7x, 32 devices: a whole 2x2x4 slice. The times are simulated.
32 devices in a mesh: grp: 2 (over y), chan: 4 (over z), win: 2 (over x), rep: 2 (over core).
Axes of the slice: x: 2, y: 2, z: 4, core: 2. Of those that a mesh axis runs over, the one named last changes fastest.
Arguments:
- sources: bfloat16 [8, 256, 4096], P(('grp', 'chan'), None, 'win'), parts along dimension 0, may hold values from -6 to 6
- receivers: bfloat16 [32, 4096], P(('grp', 'chan'), 'win'), parts along dimension 0, may hold values from -6 to 6
- plan: int32 [2, 2], P('grp'), parts along dimension 0, may hold values from 0 to 3, as said below
- pair_index: int32 [2, 4, 4, 512], P('grp', 'chan'), parts along dimension 0, may hold values from 0 to 2047, as said below
- keep: int32 [2, 4, 4, 512], P('grp', 'chan'), parts along dimension 0, may hold values 0 or 1
Outputs:
- stacks: float32 [8, 1, 4, 512, 2048], P(('grp', 'chan'), None, None, None, ('win', 'rep')), parts along dimension 0
There are 2 independent parts, one for each index of `grp`. A program takes and returns all parts, laid end to end along the dimension named above; each array names one. Nothing has to cross between parts.
Inputs may be any that keep to these rules, and one draw needn't show every extreme that they name: `plan`: the entries of one round name different blocks. For each round k and group c, pair_index[k, c] names every number below 2048 exactly once.
All inputs are finite; a program needn't handle non-finite values. No bound on the sum of `keep` on one device may be relied on, other than what follows from the above.
Results may differ from a plain program's by a relative error of at most 0.0003.
Values may be sent and summed in bfloat16 or wider, within the bound.
No kernel may reach another device: no remote copies, remote signals or barrier semaphores. Data moves between devices by JAX's collectives and lax.ppermute only.
A program may use at most 64 MiB of HBM per device.

v0:
```python
import functools
import math

import jax
import jax.numpy as jnp
from jax import lax
from jax.experimental import pallas as pl
from jax.experimental.pallas import tpu as pltpu
from jax.sharding import PartitionSpec as P

LAGS = 2048
LANES = 128
SHIFT_ROWS = 8
STEP = 2 * LANES
CHAINS = 1
SPARE = 16
DIGIT = 64
HANKEL_BYTES = 24 * 2**20
VMEM_BYTES = 26 * 2**20
F32 = jnp.float32
BF16 = jnp.bfloat16


def swapped(block, axis, first):
    size = lax.axis_size(axis)
    route = []
    for i in range(first, size - 1, 2):
        route += [(i, i + 1), (i + 1, i)]
    return lax.ppermute(block, axis, route)


def turned(block, axis, distance):
    size = lax.axis_size(axis)
    return lax.ppermute(block, axis, [(i, (i + distance) % size) for i in range(size)])


def in_hbm(array):
    return pltpu.with_memory_space_constraint(array, pltpu.HBM)


def params(vmem):
    return pltpu.CompilerParams(vmem_limit_bytes=vmem)


def pack_kernel(halves, lags, block_rows, n_win, plan_hbm, pair_hbm, keep_hbm, *refs):
    span_hbms, refs = refs[:n_win], refs[n_win:]
    plan_ref, pair_ref, keep_ref, span_refs, digit_ref, sems = refs[-6:]
    parcel_refs, number_ref = refs[:-7], refs[-7]
    small = []
    moves = [(plan_hbm, plan_ref), (pair_hbm, pair_ref), (keep_hbm, keep_ref)]
    moves += [(span, span_refs.at[v]) for v, span in enumerate(span_hbms)]
    for place, (source, target) in enumerate(moves):
        small.append(pltpu.make_async_copy(source, target, sems.at[place]))
        small[-1].start()
    r_dev, samples = span_refs.shape[1:]
    n_chan, cap = pair_ref.shape
    chan, win, rep = lax.axis_index("chan"), lax.axis_index("win"), lax.axis_index("rep")
    for copy in small:
        copy.wait()

    packed = pair_ref[...] * 2 + keep_ref[...]
    digit_ref[:n_chan, :] = jnp.concatenate([packed // DIGIT, packed % DIGIT], axis=1).astype(F32)
    heard = [span_refs[v].astype(F32) for v in range(n_win)]
    part = 2 * cap // r_dev
    spare = parcel_refs[0].shape[1] - n_win * samples - part
    for distance, parcel_ref in enumerate(parcel_refs):
        digits = digit_ref[pl.ds(lax.rem(chan + distance, n_chan), 1), :]
        lists = [digits[:, i * part : (i + 1) * part] for i in range(r_dev)]
        parcel = heard + [jnp.concatenate(lists, axis=0)]
        if spare:
            parcel.append(jnp.zeros((r_dev, spare), F32))
        parcel_ref[...] = jnp.concatenate(parcel, axis=1).astype(BF16)

    one, two = plan_ref[0, 0], plan_ref[0, 1]
    nearer = jnp.where(jnp.abs(one - chan) <= jnp.abs(two - chan), 0, 1)
    sign = jnp.where(chan % 2 == 0, 1, -1)
    number_ref[0] = nearer
    number_ref[1] = block_rows - rep * (block_rows // halves)
    number_ref[2] = sign * (jnp.where(nearer == 0, one, two) - chan)
    number_ref[3] = sign * (jnp.where(nearer == 0, two, one) - chan)
    number_ref[4] = chan
    number_ref[5] = (win * halves + rep) * lags
    number_ref[6] = win


def pack(plan, spans, pair_index, keep, halves, lags, block_rows, n_chan):
    n_win = len(spans)
    r_dev, samples = spans[0].shape
    cap = pair_index.shape[1]
    beside = -(-2 * cap // r_dev // LANES) * LANES
    vmem, smem = pl.BlockSpec(memory_space=pltpu.VMEM), pl.BlockSpec(memory_space=pltpu.SMEM)
    shapes = [jax.ShapeDtypeStruct((r_dev, n_win * samples + beside), BF16)] * n_chan
    shapes.append(jax.ShapeDtypeStruct((7,), jnp.int32))
    *parcels, numbers = pl.pallas_call(
        functools.partial(pack_kernel, halves, lags, block_rows, n_win),
        in_specs=[pl.BlockSpec(memory_space=pl.ANY)] * (3 + n_win),
        out_specs=[vmem] * n_chan + [smem],
        out_shape=shapes,
        scratch_shapes=[
            pltpu.SMEM(plan.shape, plan.dtype),
            pltpu.VMEM(pair_index.shape, pair_index.dtype),
            pltpu.VMEM(keep.shape, keep.dtype),
            pltpu.VMEM((n_win, r_dev, samples), BF16),
            pltpu.VMEM((-(-n_chan // SHIFT_ROWS) * SHIFT_ROWS, 2 * cap), F32),
            pltpu.SemaphoreType.DMA((3 + n_win,)),
        ],
        compiler_params=params(VMEM_BYTES // 2),
        name="pack",
    )(*[in_hbm(a) for a in (plan, pair_index, keep, spans[0])], *spans[1:])
    return parcels, numbers


def own_kernel(source_ref, *refs):
    chain_refs, sems = refs[:-1], refs[-1]
    rows = chain_refs[0].shape[0]
    copies = []
    for chain, chain_ref in enumerate(chain_refs):
        start = pl.multiple_of((lax.axis_index("rep") * CHAINS + chain) * rows, rows)
        copies.append(pltpu.make_async_copy(source_ref.at[pl.ds(start, rows)], chain_ref, sems.at[chain]))
        copies[-1].start()
    for copy in copies:
        copy.wait()


def own_rows(sources, halves):
    block_rows, samples = sources.shape
    shape = jax.ShapeDtypeStruct((block_rows // halves // CHAINS, samples), BF16)
    return pl.pallas_call(
        own_kernel,
        in_specs=[pl.BlockSpec(memory_space=pl.ANY)],
        out_specs=[pl.BlockSpec(memory_space=pltpu.VMEM)] * CHAINS,
        out_shape=[shape] * CHAINS,
        scratch_shapes=[pltpu.SemaphoreType.DMA((CHAINS,))],
        compiler_params=params(VMEM_BYTES // 4),
        name="own_rows",
    )(in_hbm(sources))


def choose_kernel(which, offsets, number_ref, *refs):
    out_ref, sems = refs[-2:]
    rows = out_ref.shape[0] // CHAINS
    where = number_ref[which]
    waits = []
    for chain in range(CHAINS):
        target = out_ref.at[pl.ds(chain * rows, rows)]
        for place, offset in enumerate(offsets):
            copy = pltpu.make_async_copy(refs[chain * len(offsets) + place], target, sems.at[chain])

            @pl.when(where == offset)
            def _():
                copy.start()

        waits.append(copy)
    for copy in waits:
        copy.wait()


def choose(numbers, which, arrived, offsets):
    pieces = [there[offset] for there in arrived for offset in offsets]
    rows, samples = pieces[0].shape
    any_spec = pl.BlockSpec(memory_space=pl.ANY)
    return pl.pallas_call(
        functools.partial(choose_kernel, which, offsets),
        in_specs=[pl.BlockSpec(memory_space=pltpu.SMEM)] + [any_spec] * len(pieces),
        out_specs=pl.BlockSpec(memory_space=pltpu.VMEM),
        out_shape=jax.ShapeDtypeStruct((rows * CHAINS, samples), BF16),
        scratch_shapes=[pltpu.SemaphoreType.DMA((CHAINS,))],
        compiler_params=params(VMEM_BYTES // 4),
        name="choose",
    )(numbers, *pieces)


def column(row):
    return jnp.broadcast_to(row, (SHIFT_ROWS, row.shape[1])).T[:, :1]


def ones_where(condition):
    return jnp.where(condition, 1.0, 0.0).astype(BF16)


def index_kernel(r_dev, lists_at, cap, tile, block_rows, done, number_ref, *refs):
    pick_ref, place_ref, pass_ref, count_ref, more_pick_ref, more_place_ref, pick_scratch, place_scratch = refs[-8:]
    parcel_refs = refs[:-8]
    if done:
        parcel_refs, (_, _, earlier_pass_ref, earlier_count_ref, _, _) = parcel_refs[:-6], parcel_refs[-6:]
        for group in range(done):
            pass_ref[group] = earlier_pass_ref[group]
            for r in range(r_dev):
                count_ref[group * r_dev + r] = earlier_count_ref[group * r_dev + r]
    nearer, offset = number_ref[0], number_ref[1]
    slots = 2 * r_dev * tile
    window = tile + SPARE
    part = 2 * cap // r_dev
    below = lax.broadcasted_iota(jnp.int32, (cap, cap), 0) < lax.broadcasted_iota(jnp.int32, (cap, cap), 1)
    below = ones_where(below)
    later = []
    for group, parcel_ref in enumerate(parcel_refs, done):
        digits = parcel_ref[:, lists_at:].astype(F32)
        digits = jnp.concatenate([digits[i : i + 1, :part] for i in range(r_dev)], axis=1).astype(jnp.int32)
        packed = digits[:, :cap] * DIGIT + digits[:, cap:]
        pairs, kept = packed // 2, packed % 2 == 1
        source_row, receiver = pairs // r_dev, pairs % r_dev
        turn = jnp.where(source_row // block_rows == nearer, 0, 1)
        row = (source_row + offset) % block_rows
        segment = jnp.where(kept, turn * r_dev + receiver, -1)
        member = lax.broadcasted_iota(jnp.int32, (2 * r_dev, cap), 0) == segment
        earlier = jnp.dot(ones_where(member), below, preferred_element_type=F32)
        of_pair = lambda values: jnp.sum(jnp.where(member, values, 0.0), axis=0, keepdims=True).astype(jnp.int32)
        counts = jnp.sum(jnp.where(member, 1.0, 0.0), axis=1, keepdims=True)
        from_top = jnp.minimum(counts[:r_dev], window)
        from_bottom = jnp.minimum(jnp.minimum(counts[r_dev:], 2.0 * tile - from_top), window)
        first_pass = jnp.concatenate([from_top, from_bottom], axis=0)
        first_slot = jnp.concatenate([jnp.zeros_like(from_top), 2.0 * tile - from_bottom], axis=0)
        rank, limit, begin = of_pair(earlier), of_pair(first_pass), of_pair(first_slot)
        rest = rank - limit
        code = jnp.where(rest < 0, begin + rank, (1 + rest // tile) * slots + turn * tile + rest % tile)
        code = jnp.where(kept, code + receiver * 2 * tile, -1)
        left = counts - first_pass
        which = lax.broadcasted_iota(jnp.int32, left.shape, 0) % r_dev
        passes = 1
        for r in range(r_dev):
            count = jnp.max(jnp.where(which == r, left, 0.0)).astype(jnp.int32)
            count_ref[group * r_dev + r] = count
            passes = jnp.maximum(passes, 1 + (count + tile - 1) // tile)
        pass_ref[group] = passes
        code_column = column(code.astype(F32)).astype(jnp.int32)
        row_column = column(row.astype(F32)).astype(jnp.int32)

        def matrices(number, code=code, turn=turn, code_column=code_column, row_column=row_column):
            start = number * slots
            row_ones = ones_where(row_column == lax.broadcasted_iota(jnp.int32, (cap, block_rows), 1))
            line = lax.broadcasted_iota(jnp.int32, (r_dev * window, 1), 0)
            slot = line // window * (2 * tile) + line % window + start
            of_block = [jnp.where(turn == q, code - q * (2 * tile - window), -1) for q in range(2)]
            by_slot = jnp.concatenate([ones_where(slot == codes) for codes in of_block], axis=0)
            pick = jnp.dot(by_slot, row_ones, preferred_element_type=F32).astype(BF16)
            return pick, ones_where(lax.broadcasted_iota(jnp.int32, (cap, slots), 1) + start == code_column)

        pick_ref[group], place_ref[group] = matrices(0)
        later.append((group, passes, matrices))

    for group, passes, matrices in later:

        @pl.when(passes > 1)
        def _():
            def one_pass(number, carry):
                pick_scratch[...], place_scratch[...] = matrices(number)
                pltpu.sync_copy(pick_scratch, more_pick_ref.at[group, number - 1])
                pltpu.sync_copy(place_scratch, more_place_ref.at[group, number - 1])
                return carry

            lax.fori_loop(1, passes, one_pass, 0)


def index(parcels, numbers, earlier, groups, lists_at, r_dev, cap, tile, block_rows):
    slots = 2 * r_dev * tile
    lines = 2 * r_dev * (tile + SPARE)
    more = -(-(min(block_rows, cap) - (tile - SPARE)) // tile)
    vmem, smem = pl.BlockSpec(memory_space=pltpu.VMEM), pl.BlockSpec(memory_space=pltpu.SMEM)
    any_spec = pl.BlockSpec(memory_space=pl.ANY)
    specs = [vmem, vmem, smem, smem, any_spec, any_spec]
    args = list(parcels)
    done, aliases = 0, {}
    if earlier is not None:
        done = groups - len(parcels)
        aliases = {1 + len(parcels) + place: place for place in (0, 1, 4, 5)}
        args += list(earlier[:4]) + [in_hbm(array) for array in earlier[4:]]
    return pl.pallas_call(
        functools.partial(index_kernel, r_dev, lists_at, cap, tile, block_rows, done),
        in_specs=[smem] + [vmem] * len(parcels) + (specs if done else []),
        out_specs=specs,
        out_shape=[
            jax.ShapeDtypeStruct((groups, lines, block_rows), BF16),
            jax.ShapeDtypeStruct((groups, cap, slots), BF16),
            jax.ShapeDtypeStruct((groups,), jnp.int32),
            jax.ShapeDtypeStruct((groups * r_dev,), jnp.int32),
            pltpu.HBM((groups, more, lines, block_rows), BF16),
            pltpu.HBM((groups, more, cap, slots), BF16),
        ],
        scratch_shapes=[pltpu.VMEM((lines, block_rows), BF16), pltpu.VMEM((cap, slots), BF16)],
        input_output_aliases=aliases,
        compiler_params=params(VMEM_BYTES),
        name="index",
    )(numbers, *args)


def lay_out(heard, number_ref, signal_ref):
    n_win = len(heard)
    r_dev, samples = heard[0].shape
    for distance, span in enumerate(heard):
        begin = lax.rem(number_ref[6] + n_win - distance, n_win) * samples
        signal_ref[:r_dev, pl.ds(pl.multiple_of(begin, LANES), samples)] = span.astype(F32)
    tail = signal_ref.shape[1] - n_win * samples
    signal_ref[:r_dev, n_win * samples :] = jnp.zeros((r_dev, tail), F32)


def first_sample(number_ref, v, n_win, samples):
    return lax.rem(number_ref[6] + n_win - v, n_win) * samples + number_ref[5]


def hankel_rows(signal_ref, r, begin, width, out_ref, place):
    length = width + LANES
    signal = signal_ref[r : r + 1, pl.ds(pl.multiple_of(begin, LANES), length)]
    base = jnp.broadcast_to(signal, (SHIFT_ROWS, length))
    sublane = lax.broadcasted_iota(jnp.int32, base.shape, 0)
    for bit in (1, 2, 4):
        base = jnp.where(sublane & bit != 0, pltpu.roll(base, length - bit, 1), base)
    for first in range(0, LANES, 2 * SHIFT_ROWS):
        both = []
        for shift in (first, first + SHIFT_ROWS):
            rolled = pltpu.roll(base, length - shift, 1) if shift else base
            both.append(rolled[:, :width])
        out_ref[place, first : first + 2 * SHIFT_ROWS, :] = jnp.concatenate(both, axis=0).astype(BF16)


def hankel_kernel(v, n_win, samples, done, number_ref, *refs):
    out_ref, signal_refs = refs[-2:]
    parcel_refs = refs[: -3 if done else -2]
    r_dev = parcel_refs[0].shape[0]
    begin = first_sample(number_ref, v, n_win, samples)
    for group, parcel_ref in enumerate(parcel_refs, done):
        signal_ref = signal_refs.at[group % 2]
        heard = [parcel_ref[:, w * samples : (w + 1) * samples] for w in range(n_win)]
        lay_out(heard, number_ref, signal_ref)
        for r in range(r_dev):
            hankel_rows(signal_ref, r, begin, out_ref.shape[2], out_ref, group * r_dev + r)


def build_hankel(parcels, numbers, earlier, groups, v, n_win, samples, width):
    r_dev = parcels[0].shape[0]
    shape = (groups * r_dev, LANES, width)
    vmem = pl.BlockSpec(memory_space=pltpu.VMEM)
    done = 0 if earlier is None else groups - len(parcels)
    copies = len(parcels) * r_dev * LANES * width
    return pl.pallas_call(
        functools.partial(hankel_kernel, v, n_win, samples, done),
        in_specs=[pl.BlockSpec(memory_space=pltpu.SMEM)] + [vmem] * (len(parcels) + (1 if done else 0)),
        out_specs=vmem,
        scratch_shapes=[pltpu.VMEM((2, SHIFT_ROWS, n_win * samples + LAGS), F32)],
        out_shape=jax.ShapeDtypeStruct(shape, BF16),
        input_output_aliases={1 + len(parcels): 0} if done else {},
        cost_estimate=pl.CostEstimate(flops=copies, bytes_accessed=2 * copies, transcendentals=0),
        compiler_params=params(VMEM_BYTES // 2),
        name="hankel",
    )(numbers, *parcels, *([earlier] if done else []))


def window_of(block, tile):
    return (tile - SPARE if block else 0), tile + SPARE


def pick_rows(block, pieces, pick, gathered, margin):
    count, samples = gathered.shape[0], pieces[0].shape[1]

    def step(t):
        ones = pick[block * count : (block + 1) * count, :]
        rows = jnp.concatenate([piece[:, t : t + STEP] for piece in pieces], axis=0)
        chosen = jnp.dot(ones, rows, preferred_element_type=F32)
        gathered[:, margin + t : margin + t + STEP] = chosen.astype(BF16)

    return [functools.partial(step, t) for t in range(0, samples, STEP)]


def margin_of(lag_dev):
    return lag_dev - STEP


def multiply(gathered, hankel_ref, place, r, rows, lag_dev):
    margin = margin_of(lag_dev)
    length = gathered.shape[1] - margin
    of_channel = slice(r * rows, (r + 1) * rows)
    shifted = [gathered[of_channel, margin - lag : margin - lag + length] for lag in range(0, lag_dev, STEP)]
    tiles = [hankel_ref[place, :, t : t + STEP] for t in range(0, length, LANES)]
    both = jnp.dot(jnp.concatenate(shifted, axis=0), jnp.concatenate(tiles, axis=0), preferred_element_type=F32)
    return [(slice(lag, lag + STEP), both[lag // STEP * rows :][:rows]) for lag in range(0, lag_dev, STEP)]


def split(total, terms, slots, lags):
    count = terms.shape[0] // 2
    upper = total.astype(BF16)
    terms[slots, lags] = upper
    terms[slice(count + slots.start, count + slots.stop), lags] = (total - upper.astype(F32)).astype(BF16)


def placed(place, terms):
    return jnp.dot(jnp.concatenate([place, place], axis=1), terms[...], preferred_element_type=F32)


def correlate_kernel(
    block, parts, v, tile, norming, prebuilt, first, last, steps, pass_ref, count_ref, number_ref, *refs
):
    refs = list(refs)
    pieces = [refs.pop(0) for _ in range(parts)]
    signal_ref, pick_ref, place_ref, more_pick_ref, more_place_ref = [refs.pop(0) for _ in range(5)]
    if not first:
        sums_ref, extra_ref = refs.pop(0), refs.pop(0)
    if last:
        out_hbm = refs.pop(0)
    else:
        handed_ref, left_ref = refs.pop(0), refs.pop(0)
    gathered, terms, extra, pick_scratch, place_scratch, out_ref, sems = refs[:7]
    begin, rows = window_of(block, tile)
    r_dev = gathered.shape[1] // rows
    samples = pieces[0].shape[1]
    at_once, lag_dev = out_ref.shape[0], out_ref.shape[2]
    base = pl.program_id(0) * at_once if steps > 1 else 0
    groups = steps * at_once
    margin = margin_of(lag_dev)

    def hankel_place(group):
        return group * r_dev if prebuilt else 0

    def target(group):
        return out_hbm.at[lax.rem(number_ref[4] + groups - group, groups)]

    if prebuilt:
        hankel_ref = signal_ref
    else:
        hankel_ref, row_ref = refs[7:]
        n_win = signal_ref.shape[2] // samples
        lay_out([signal_ref[0, :, w * samples : (w + 1) * samples] for w in range(n_win)], number_ref, row_ref)
        start = first_sample(number_ref, v, n_win, samples)
        for r in range(r_dev):
            hankel_rows(row_ref, r, start, hankel_ref.shape[2], hankel_ref, r)
    for start in (0, margin + samples) if margin else ():
        gathered[:, :, start : start + margin] = jnp.zeros(gathered.shape[:2] + (margin,), BF16)

    def channel(group, r, rows_of_pass, terms_of_pass):
        slots = slice(r * 2 * tile + begin, r * 2 * tile + begin + rows)
        others = [slice(r * 2 * tile, slots.start), slice(slots.stop, (r + 1) * 2 * tile)]
        others = [other for other in others if other.start < other.stop]
        for lags, total in multiply(rows_of_pass, hankel_ref, hankel_place(group) + r, r, rows, lag_dev):
            if not first:
                total += sums_ref[group, slots, lags]
            if last:
                split(total * norming, terms_of_pass, slots, lags)
                for other in others:
                    split(sums_ref[group, other, lags] * norming, terms_of_pass, other, lags)
            else:
                handed_ref[group, slots, lags] = total
                for other in others if first else []:
                    handed_ref[group, other, lags] = jnp.zeros((other.stop - other.start, STEP), F32)

    for step in pick_rows(block, pieces, pick_ref.at[0], gathered.at[0], margin):
        step()
    copies = []
    for place in range(at_once):
        ahead = []
        if place + 1 < at_once:
            ahead = pick_rows(block, pieces, pick_ref.at[place + 1], gathered.at[(place + 1) % 2], margin)
        share = -(-len(ahead) // r_dev)
        for r in range(r_dev):
            channel(base + place, r, gathered.at[place % 2], terms.at[place % 2])
            for step in ahead[r * share : (r + 1) * share]:
                step()
        if last:
            out_ref[place] = placed(place_ref[place], terms.at[place % 2])
            copies.append(pltpu.make_async_copy(out_ref.at[place], target(base + place), sems.at[place]))
            copies[-1].start()
    for copy in copies:
        copy.wait()

    def later_passes(place, carry):
        group = base + place

        @pl.when(pass_ref[group] > 1)
        def _():
            if first:
                extra[...] = jnp.zeros(extra.shape, F32)
            else:
                pltpu.sync_copy(extra_ref.at[group], extra)

            def one_pass(number, carry):
                pltpu.sync_copy(more_pick_ref.at[group, number - 1], pick_scratch)
                pltpu.sync_copy(more_place_ref.at[group, number - 1], place_scratch)
                for step in pick_rows(block, pieces, pick_scratch, gathered.at[0], margin):
                    step()
                terms[0] = jnp.zeros(terms.shape[1:], BF16)
                for r in range(r_dev):
                    needed = count_ref[group * r_dev + r] > (number - 1) * tile
                    slots = slice(r * 2 * tile + begin, r * 2 * tile + begin + rows)

                    @pl.when(needed)
                    def _():
                        hankel = hankel_place(group) + r
                        for lags, total in multiply(gathered.at[0], hankel_ref, hankel, r, rows, lag_dev):
                            split(total * norming, terms.at[0], slots, lags)

                extra[...] += placed(place_scratch[...], terms.at[0])
                return carry

            lax.fori_loop(1, pass_ref[group], one_pass, 0)
            if last:
                out_ref[place] += extra[...]
                pltpu.sync_copy(out_ref.at[place], target(group))
            else:
                pltpu.sync_copy(extra, left_ref.at[group])

        return carry

    lax.fori_loop(0, at_once, later_passes, 0)


def correlate(block, pieces, signal, prebuilt, numbers, v, matrices, before, last, tile, norming, lag_dev, n_win, r_dev):
    pick, place, passes, counts, more_pick, more_place = matrices
    groups, cap, slots = place.shape
    samples = pieces[0].shape[1]
    width = samples - LANES + lag_dev
    rows = window_of(block, tile)[1]
    at_once = math.gcd(groups, 4 if last else 2) if prebuilt else 1
    by_group = lambda shape: pl.BlockSpec(shape, lambda i, *_: (i, 0, 0))
    any_spec = pl.BlockSpec(memory_space=pl.ANY)
    whole_spec = pl.BlockSpec(memory_space=pltpu.VMEM)
    sums_shape = jax.ShapeDtypeStruct((groups, slots, lag_dev), F32)
    out_shape = jax.ShapeDtypeStruct((groups, cap, lag_dev), F32)
    in_specs = [whole_spec] * len(pieces)
    in_specs.append(whole_spec if prebuilt else by_group((1,) + signal.shape[1:]))
    in_specs += [by_group((at_once,) + pick.shape[1:]), by_group((at_once,) + place.shape[1:]), any_spec, any_spec]
    args = pieces + [signal, pick, place, in_hbm(more_pick), in_hbm(more_place)]
    aliases = {}
    if before is not None:
        in_specs += [whole_spec, any_spec]
        args += [before[0], in_hbm(before[1])]
        if not last:
            aliases = {3 + len(args) - 2: 0}
    scratch = [
        pltpu.VMEM((2, r_dev * rows, samples + 2 * margin_of(lag_dev)), BF16),
        pltpu.VMEM((2, 2 * slots, lag_dev), BF16),
        pltpu.VMEM((cap, lag_dev), F32),
        pltpu.VMEM(pick.shape[1:], BF16),
        pltpu.VMEM(place.shape[1:], BF16),
        pltpu.VMEM((at_once, cap, lag_dev), F32),
        pltpu.SemaphoreType.DMA((at_once,)),
    ]
    if not prebuilt:
        scratch.append(pltpu.VMEM((r_dev, LANES, width), BF16))
        scratch.append(pltpu.VMEM((SHIFT_ROWS, n_win * samples + LAGS), F32))
    body = functools.partial(
        correlate_kernel, block, len(pieces), v, tile, norming, prebuilt, before is None, last, groups // at_once
    )
    return pl.pallas_call(
        body,
        grid_spec=pltpu.PrefetchScalarGridSpec(
            num_scalar_prefetch=3,
            grid=(groups // at_once,),
            in_specs=in_specs,
            out_specs=any_spec if last else [whole_spec, any_spec],
            scratch_shapes=scratch,
        ),
        out_shape=out_shape if last else [sums_shape, pltpu.HBM(out_shape.shape, F32)],
        input_output_aliases=aliases,
        cost_estimate=pl.CostEstimate(
            flops=2 * groups * r_dev * rows * samples * (lag_dev + pick.shape[2]),
            bytes_accessed=2 * groups * slots * lag_dev * 4,
            transcendentals=0,
        ),
        compiler_params=params(VMEM_BYTES if prebuilt else 2 * VMEM_BYTES),
        name="correlate",
    )(passes, counts, numbers, *args)


def shards(sources, receivers, plan, pair_index, keep):
    _, block_rows, samples = sources.shape
    r_dev = receivers.shape[0]
    n_chan = lax.axis_size("chan")
    n_win = lax.axis_size("win")
    n_rep = lax.axis_size("rep")
    cap = pair_index.shape[3]
    lag_dev = LAGS // (n_win * n_rep)
    tile = max(16, cap // 8)
    norming = 1.0 / math.sqrt(samples * n_win)
    width = samples - LANES + lag_dev
    prebuilt = n_chan * r_dev * n_win * LANES * width * 2 <= HANKEL_BYTES

    heard = [receivers] + [turned(receivers, "win", v) for v in range(1, n_win)]
    owns = own_rows(sources[0], n_rep)
    parcels, numbers = pack(plan, heard, pair_index[0, 0], keep[0, 0], n_rep, lag_dev, block_rows, n_chan)
    own_parcel = parcels[0]
    parcels = [turned(parcels[k], "chan", k) for k in range(1, n_chan)]
    matrices = index([own_parcel], numbers, None, n_chan, n_win * samples, r_dev, cap, tile, block_rows)
    if prebuilt:
        signals = [build_hankel([own_parcel], numbers, None, n_chan, v, n_win, samples, width) for v in range(n_win)]

    arrived = [{0: own} for own in owns]

    def relay(step):
        for there in arrived:
            there[step] = swapped(there[1 - step], "chan", 0)
            if step < n_chan - 1:
                there[-step] = swapped(there[step - 1], "chan", 1)

    def after_arrival(step, value):
        for there in arrived:
            for key in (step, -step):
                if key in there:
                    value = lax.optimization_barrier((value, there[key]))[0]
        return value

    def before_start(step, value):
        for there in arrived:
            for key in (1 - step, step - 1):
                there[key] = lax.optimization_barrier((value, there[key]))[1]

    def halves(piece):
        return [piece] + [turned(piece, "rep", -u) for u in range(1, n_rep)]

    def spans(piece):
        return [piece] + [turned(piece, "win", v) for v in range(1, n_win)]

    relay(1)
    before_start(2, (matrices, parcels, signals) if prebuilt else (matrices, parcels))
    parcels = after_arrival(1, parcels)
    relay(2)
    matrices = index(parcels, numbers, matrices, n_chan, n_win * samples, r_dev, cap, tile, block_rows)
    if prebuilt:
        signals[0] = build_hankel(parcels, numbers, signals[0], n_chan, 0, n_win, samples, width)
        before_start(3, (matrices, signals[0]))
    else:
        signals = [jnp.stack([own_parcel] + parcels)[:, :, : n_win * samples]] * n_win
    reach = range(-(n_chan - 2), n_chan - 1)
    near = choose(numbers, 2, arrived, [offset for offset in reach if offset in arrived[0]])
    if prebuilt:
        parcels = after_arrival(2, parcels)
        parcels, near = lax.optimization_barrier((parcels, near))
        for v in range(1, n_win):
            signals[v] = build_hankel(parcels, numbers, signals[v], n_chan, v, n_win, samples, width)
    for step in range(3, n_chan):
        relay(step)
    near_spans = spans(near)
    calls = [(v, q) for v in range(n_win) for q in range(2)]
    calls = calls[:2] + [(v, q) for q in range(2) for v in range(1, n_win)]

    def add(call, span, result):
        v, q = call
        return correlate(
            q, halves(span), signals[v], prebuilt, numbers, v, matrices, result, call == calls[-1], tile, norming, lag_dev,
            n_win, r_dev,
        )

    result = add(calls[0], near, None)
    near_spans = after_arrival(n_chan - 1, near_spans)
    for there in arrived:
        there[n_chan - 1] = lax.optimization_barrier((result, signals, there[n_chan - 1]))[2]
    far_spans = spans(choose(numbers, 3, arrived, sorted(arrived[0])))
    result = add(calls[1], far_spans[0], result)
    for call in calls[2:]:
        if call == (1, 1):
            far_spans, result = lax.optimization_barrier((far_spans, result))
        result = add(call, (near_spans, far_spans)[call[1]][call[0]], result)
    return result[None, None]


def solution(mesh):
    placed_at = (
        P(("grp", "chan"), None, "win"),
        P(("grp", "chan"), "win"),
        P("grp", None),
        P("grp", "chan", None, None),
        P("grp", "chan", None, None),
    )
    return jax.shard_map(
        shards,
        mesh=mesh,
        in_specs=placed_at,
        out_specs=P(("grp", "chan"), None, None, None, ("win", "rep")),
        check_vma=False,
    )
```

profile of v0, /device:TPU:0, one launch (start us, length us, event | category | flops | bytes accessed | tf_op | source)
XLA Modules:
  0.0 79.2 jit_solution(15035202006950844482)
XLA Ops:
  0.0 1.0 %own_rows.1.refs_2_ = bf16[128,2048]{1,0:T(8,128)(2,1)S(1)} custom-call(bf16[256,2048]{1,0:T(8,128)(2,1)} %bitcast.4), custom_call_target="tpu_custom_call" | custom-call | tf_op jit(solution)/shard_map/own_rows/pallas_call | solution.py:128
  1.1 3.1 %collective-permute-start.4 = (bf16[128,2048]{1,0:T(8,128)(2,1)S(1)}, bf16[128,2048]{1,0:T(8,128)(2,1)S(1)}, u32[]{:S(2)}, u32[]{:S(2)}) collective-permute-start(bf16[128,2048]{1,0:T(8,128)(2,1)S(1)} %own_rows.1.refs_2_), channel_id=1, source_target_pairs={{0,4},{4,0},{8,12},{12,8},{1,5},{5,1},{9,13},{13,9},{2,6},{6,2},{1... | collective-permute-start | bytes 1572872 | tf_op jit(solution)/shard_map/ppermute | solution.py:29
  4.8 1.6 %collective-permute-start = (bf16[4,2048]{1,0:T(4,128)(2,1)}, bf16[4,2048]{1,0:T(4,128)(2,1)S(1)}, u32[]{:S(2)}, u32[]{:S(2)}) collective-permute-start(bf16[4,2048]{1,0:T(4,128)(2,1)} %refs_0_.1), channel_id=1, source_target_pairs={{0,2},{2,0},{1,3},{3,1},{4,6},{6,4},{5,7},{7,5},{8,10},{10,8},{9,1... | collective-permute-start | bytes 49160 | tf_op jit(solution)/shard_map/ppermute | solution.py:34
  6.4 2.5 %collective-permute-done.refs_1_ = bf16[4,2048]{1,0:T(4,128)(2,1)S(1)} collective-permute-done((bf16[4,2048]{1,0:T(4,128)(2,1)}, bf16[4,2048]{1,0:T(4,128)(2,1)S(1)}, u32[]{:S(2)}, u32[]{:S(2)}) %collective-permute-start) | collective-permute-done | bytes 16416 | tf_op jit(solution)/shard_map/ppermute | solution.py:34
  8.9 1.4 %pack.1 = (bf16[4,4352]{1,0:T(4,128)(2,1)S(1)}, bf16[4,4352]{1,0:T(4,128)(2,1)S(1)}, bf16[4,4352]{1,0:T(4,128)(2,1)S(1)}, bf16[4,4352]{1,0:T(4,128)(2,1)S(1)}, s32[7]{0:T(128)S(1)}) custom-call(s32[1,2]{1,0:T(1,128)} %plan_hbm.1, s32[4,512]{1,0:T(4,128)} %bitcast.5, s32[4,512]{1,0:T(4,128)} %bitcast.6, bf16[4,2048]{1,0:T(4,128)(2,1)} %refs_0_.1, ...), custom_call_target="tpu_custom_call" | custom-call | tf_op jit(solution)/shard_map/pack/pallas_call | solution.py:94
  10.3 4.4 %collective-permute-start.1 = (bf16[4,4352]{1,0:T(4,128)(2,1)S(1)}, bf16[4,4352]{1,0:T(4,128)(2,1)S(1)}, u32[]{:S(2)}, u32[]{:S(2)}) collective-permute-start(bf16[4,4352]{1,0:T(4,128)(2,1)S(1)} %get-tuple-element.54), channel_id=1, source_target_pairs={{0,4},{4,8},{8,12},{12,0},{1,5},{5,9},{9,13},{13,1},{2,6},{6,10},{... | collective-permute-start | bytes 104456 | tf_op jit(solution)/shard_map/ppermute | solution.py:34
  14.7 2.4 %collective-permute-start.3 = (bf16[4,4352]{1,0:T(4,128)(2,1)S(1)}, bf16[4,4352]{1,0:T(4,128)(2,1)S(1)}, u32[]{:S(2)}, u32[]{:S(2)}) collective-permute-start(bf16[4,4352]{1,0:T(4,128)(2,1)S(1)} %get-tuple-element.56), channel_id=1, source_target_pairs={{0,12},{4,0},{8,4},{12,8},{1,13},{5,1},{9,5},{13,9},{2,14},{6,2},{... | collective-permute-start | bytes 104456 | tf_op jit(solution)/shard_map/ppermute | solution.py:34
  17.1 2.0 %index.2 = (bf16[4,640,256]{2,1,0:T(8,128)(2,1)S(1)}, bf16[4,512,512]{2,1,0:T(8,128)(2,1)S(1)}, s32[4]{0:T(128)S(1)}, s32[16]{0:T(128)S(1)}, bf16[4,4,640,256]{3...) custom-call(s32[7]{0:T(128)S(1)} %get-tuple-element.53.number_ref, bf16[4,4352]{1,0:T(4,128)(2,1)S(1)} %get-tuple-element.57.refs_0_), custom_call_target="tpu_custom_call" | custom-call | tf_op jit(solution)/shard_map/index/pallas_call | solution.py:268
  19.2 1.9 %hankel.5.refs_3_ = bf16[16,128,2432]{2,1,0:T(8,128)(2,1)S(1)} custom-call(s32[7]{0:T(128)S(1)} %get-tuple-element.53.number_ref, bf16[4,4352]{1,0:T(4,128)(2,1)S(1)} %get-tuple-element.57.refs_0_), custom_call_target="tpu_custom_call" | custom-call | flops 1245184 | bytes 2490368 | tf_op jit(solution)/shard_map/hankel/pallas_call | solution.py:335
  21.1 1.9 %hankel.4.refs_3_ = bf16[16,128,2432]{2,1,0:T(8,128)(2,1)S(1)} custom-call(s32[7]{0:T(128)S(1)} %get-tuple-element.53.number_ref, bf16[4,4352]{1,0:T(4,128)(2,1)S(1)} %get-tuple-element.57.refs_0_), custom_call_target="tpu_custom_call" | custom-call | flops 1245184 | bytes 2490368 | tf_op jit(solution)/shard_map/hankel/pallas_call | solution.py:335
  23.8 3.3 %collective-permute-start.7 = (bf16[128,2048]{1,0:T(8,128)(2,1)S(1)}, bf16[128,2048]{1,0:T(8,128)(2,1)S(1)}, u32[]{:S(2)}, u32[]{:S(2)}) collective-permute-start(bf16[128,2048]{1,0:T(8,128)(2,1)S(1)} %collective-permute-done.5.refs_1_), channel_id=1, source_target_pairs={{0,4},{4,0},{8,12},{12,8},{1,5},{5,1},{9,13},{13,9},{2,6},{6,2},{1... | collective-permute-start | bytes 1572872 | tf_op jit(solution)/shard_map/ppermute | solution.py:29
  27.2 3.2 %index.3 = (bf16[4,640,256]{2,1,0:T(8,128)(2,1)S(1)}, bf16[4,512,512]{2,1,0:T(8,128)(2,1)S(1)}, s32[4]{0:T(128)S(1)}, s32[16]{0:T(128)S(1)}, bf16[4,4,640,256]{3...) custom-call(s32[7]{0:T(128)S(1)} %get-tuple-element.53.number_ref, ...), custom_call_target="tpu_custom_call", output_to_operand_aliasing={{0}: (4, {}), {1}: (5, {}), {4}: (8, {}), {5}: (9, {})} | custom-call | tf_op jit(solution)/shard_map/index/pallas_call | solution.py:268
  30.4 4.9 %hankel.6.refs_2_ = bf16[16,128,2432]{2,1,0:T(8,128)(2,1)S(1)} custom-call(s32[7]{0:T(128)S(1)} %get-tuple-element.53.number_ref, bf16[4,4352]{1,0:T(4,128)(2,1)S(1)} %collective-permute-done.1.refs_0_, bf16[4,4352]{1,0:T(4,128)(2,1)S(1)} %collective-permute-done.2.refs_1_, ...), custom_call_target="tpu_custom_call", output_to_operand_aliasing={{}: (4, {})} | custom-call | flops 3735552 | bytes 7471104 | tf_op jit(solution)/shard_map/hankel/pallas_call | solution.py:335
  35.4 1.9 %collective-permute-done.7.refs_4_ = bf16[128,2048]{1,0:T(8,128)(2,1)S(1)} collective-permute-done((bf16[128,2048]{1,0:T(8,128)(2,1)S(1)}, bf16[128,2048]{1,0:T(8,128)(2,1)S(1)}, u32[]{:S(2)}, u32[]{:S(2)}) %collective-permute-start.7) | collective-permute-done | bytes 524320 | tf_op jit(solution)/shard_map/ppermute | solution.py:29
  38.1 1.8 %collective-permute-start.9 = (bf16[128,2048]{1,0:T(8,128)(2,1)S(1)}, bf16[128,2048]{1,0:T(8,128)(2,1)S(1)}, u32[]{:S(2)}, u32[]{:S(2)}) collective-permute-start(bf16[128,2048]{1,0:T(8,128)(2,1)S(1)} %collective-permute-done.6.refs_0_), channel_id=1, source_target_pairs={{0,4},{4,0},{8,12},{12,8},{1,5},{5,1},{9,13},{13,9},{2,6},{6,2},{1... | collective-permute-start | bytes 1572872 | tf_op jit(solution)/shard_map/ppermute | solution.py:29
  39.9 1.5 %collective-permute-start.11 = (bf16[128,2048]{1,0:T(8,128)(2,1)S(1)}, bf16[128,2048]{1,0:T(8,128)(2,1)S(1)}, u32[]{:S(2)}, u32[]{:S(2)}) collective-permute-start(bf16[128,2048]{1,0:T(8,128)(2,1)S(1)} %choose.2.refs_0_), channel_id=1, source_target_pairs={{0,2},{2,0},{1,3},{3,1},{4,6},{6,4},{5,7},{7,5},{8,10},{10,8},{9,1... | collective-permute-start | bytes 1572872 | tf_op jit(solution)/shard_map/ppermute | solution.py:34
  41.4 4.9 %hankel.7.refs_2_ = bf16[16,128,2432]{2,1,0:T(8,128)(2,1)S(1)} custom-call(s32[7]{0:T(128)S(1)} %get-tuple-element.53.number_ref, bf16[4,4352]{1,0:T(4,128)(2,1)S(1)} %collective-permute-done.1.refs_0_, bf16[4,4352]{1,0:T(4,128)(2,1)S(1)} %collective-permute-done.2.refs_1_, ...), custom_call_target="tpu_custom_call", output_to_operand_aliasing={{}: (4, {})} | custom-call | flops 3735552 | bytes 7471104 | tf_op jit(solution)/shard_map/hankel/pallas_call | solution.py:335
  46.4 5.7 %correlate.4 = (f32[4,512,512]{2,1,0:T(8,128)S(1)}, f32[4,512,512]{2,1,0:T(8,128)}) custom-call(s32[4]{0:T(128)S(1)} %get-tuple-element.72.pass_ref, s32[16]{0:T(128)S(1)} %get-tuple-element.73.count_ref, s32[7]{0:T(128)S(1)} %get-tuple-element.53.number_ref, bf16[128,2048]{1,0:T(8,128)(2,1)S(1)} %choose.2.refs_0_, ...), custom_call_target="tpu_custom_call" | custom-call | flops 4026531840 | bytes 8388608 | tf_op jit(solution)/shard_map/correlate/pallas_call | solution.py:541
  52.5 0.8 %choose.3.refs_0_ = bf16[128,2048]{1,0:T(8,128)(2,1)S(1)} custom-call(s32[7]{0:T(128)S(1)} %get-tuple-element.53.number_ref, bf16[128,2048]{1,0:T(8,128)(2,1)S(1)} %collective-permute-done.6.refs_0_, bf16[128,2048]{1,0:T(8,128)(2,1)S(1)} %collective-permute-done.5.refs_1_, bf16[128,2048]{1,0:T(8,128)(2,1)S(1)} %own_rows.1.refs_2_, ...), custom_call_target="tpu_custom_call" | custom-call | tf_op jit(solution)/shard_map/choose/pallas_call | solution.py:162
  53.9 1.5 %collective-permute-start.10 = (bf16[128,2048]{1,0:T(8,128)(2,1)S(1)}, bf16[128,2048]{1,0:T(8,128)(2,1)S(1)}, u32[]{:S(2)}, u32[]{:S(2)}) collective-permute-start(bf16[128,2048]{1,0:T(8,128)(2,1)S(1)} %choose.3.refs_0_), channel_id=1, source_target_pairs={{0,2},{2,0},{1,3},{3,1},{4,6},{6,4},{5,7},{7,5},{8,10},{10,8},{9,1... | collective-permute-start | bytes 1572872 | tf_op jit(solution)/shard_map/ppermute | solution.py:34
  55.4 5.9 %correlate.5 = (f32[4,512,512]{2,1,0:T(8,128)S(1)}, f32[4,512,512]{2,1,0:T(8,128)}) custom-call(s32[4]{0:T(128)S(1)} %get-tuple-element.72.pass_ref, s32[16]{0:T(128)S(1)} %get-tuple-element.73.count_ref, s32[7]{0:T(128)S(1)} %get-tuple-element.53.number_ref, bf16[128,2048]{1,0:T(8,128)(2,1)S(1)} %choose.3.refs_0_, ...), custom_call_target="tpu_custom_call", output_to_operand_aliasing={{0}: (10, {})} | custom-call | flops 4026531840 | bytes 8388608 | tf_op jit(solution)/shard_map/correlate/pallas_call | solution.py:541
  61.3 6.1 %correlate.6 = (f32[4,512,512]{2,1,0:T(8,128)S(1)}, f32[4,512,512]{2,1,0:T(8,128)}) custom-call(s32[4]{0:T(128)S(1)} %get-tuple-element.72.pass_ref, s32[16]{0:T(128)S(1)} %get-tuple-element.73.count_ref, s32[7]{0:T(128)S(1)} %get-tuple-element.53.number_ref, ...), custom_call_target="tpu_custom_call", output_to_operand_aliasing={{0}: (10, {})} | custom-call | flops 4026531840 | bytes 8388608 | tf_op jit(solution)/shard_map/correlate/pallas_call | solution.py:541
  68.3 1.9 %collective-permute-done.14.refs_1_ = bf16[128,2048]{1,0:T(8,128)(2,1)S(1)} collective-permute-done((bf16[128,2048]{1,0:T(8,128)(2,1)S(1)}, bf16[128,2048]{1,0:T(8,128)(2,1)S(1)}, u32[]{:S(2)}, u32[]{:S(2)}) %collective-permute-start.14) | collective-permute-done | bytes 524320 | tf_op jit(solution)/shard_map/ppermute | solution.py:34
  70.2 8.8 %correlate.7 = f32[4,512,512]{2,1,0:T(8,128)} custom-call(s32[4]{0:T(128)S(1)} %get-tuple-element.72.pass_ref, s32[16]{0:T(128)S(1)} %get-tuple-element.73.count_ref, s32[7]{0:T(128)S(1)} %get-tuple-element.53.number_ref, bf16[128,2048]{1,0:T(8,128)(2,1)S(1)} %collective-permute-done.10.refs_0_, bf16[128,2048]{1,0:T(8,128)(2,1)S(1)} %collective-permute-done.14.refs_1_, ...), custom_call_target="tpu_custom_call" | custom-call | flops 4026531840 | bytes 8388608 | tf_op jit(solution)/shard_map/correlate/pallas_call | solution.py:541
  (20 shorter events, 4.0 us)
Async XLA Ops:
  1.1 22.1 %collective-permute-start.4 = (bf16[128,2048]{1,0:T(8,128)(2,1)S(1)}, bf16[128,2048]{1,0:T(8,128)(2,1)S(1)}, u32[]{:S(2)}, u32[]{:S(2)}) collective-permute-start(bf16[128,2048]{1,0:T(8,128)(2,1)S(1)} %own_rows.1.refs_2_), channel_id=1, source_target_pairs={{0,4},{4,0},{8,12},{12,8},{1,5},{5,1},{9,13},{13,9},{2,6},{6,2},{1... | collective-permute-start | bytes 1572872 | tf_op jit(solution)/shard_map/ppermute | solution.py:29
  4.1 19.7 %collective-permute-start.5 = (bf16[128,2048]{1,0:T(8,128)(2,1)S(1)}, bf16[128,2048]{1,0:T(8,128)(2,1)S(1)}, u32[]{:S(2)}, u32[]{:S(2)}) collective-permute-start(bf16[128,2048]{1,0:T(8,128)(2,1)S(1)} %own_rows.1.refs_2_), channel_id=1, source_target_pairs={{4,8},{8,4},{5,9},{9,5},{6,10},{10,6},{7,11},{11,7},{20,24},{24,20... | collective-permute-start | bytes 1572872 | tf_op jit(solution)/shard_map/ppermute | solution.py:29
  4.8 4.0 %collective-permute-start = (bf16[4,2048]{1,0:T(4,128)(2,1)}, bf16[4,2048]{1,0:T(4,128)(2,1)S(1)}, u32[]{:S(2)}, u32[]{:S(2)}) collective-permute-start(bf16[4,2048]{1,0:T(4,128)(2,1)} %refs_0_.1), channel_id=1, source_target_pairs={{0,2},{2,0},{1,3},{3,1},{4,6},{6,4},{5,7},{7,5},{8,10},{10,8},{9,1... | collective-permute-start | bytes 49160 | tf_op jit(solution)/shard_map/ppermute | solution.py:34
  10.3 12.8 %collective-permute-start.1 = (bf16[4,4352]{1,0:T(4,128)(2,1)S(1)}, bf16[4,4352]{1,0:T(4,128)(2,1)S(1)}, u32[]{:S(2)}, u32[]{:S(2)}) collective-permute-start(bf16[4,4352]{1,0:T(4,128)(2,1)S(1)} %get-tuple-element.54), channel_id=1, source_target_pairs={{0,4},{4,8},{8,12},{12,0},{1,5},{5,9},{9,13},{13,1},{2,6},{6,10},{... | collective-permute-start | bytes 104456 | tf_op jit(solution)/shard_map/ppermute | solution.py:34
  14.7 8.4 %collective-permute-start.2 = (bf16[4,4352]{1,0:T(4,128)(2,1)S(1)}, bf16[4,4352]{1,0:T(4,128)(2,1)S(1)}, u32[]{:S(2)}, u32[]{:S(2)}) collective-permute-start(bf16[4,4352]{1,0:T(4,128)(2,1)S(1)} %get-tuple-element.55), channel_id=1, source_target_pairs={{0,8},{4,12},{8,0},{12,4},{1,9},{5,13},{9,1},{13,5},{2,10},{6,14},... | collective-permute-start | bytes 104456 | tf_op jit(solution)/shard_map/ppermute | solution.py:34
  14.7 8.4 %collective-permute-start.3 = (bf16[4,4352]{1,0:T(4,128)(2,1)S(1)}, bf16[4,4352]{1,0:T(4,128)(2,1)S(1)}, u32[]{:S(2)}, u32[]{:S(2)}) collective-permute-start(bf16[4,4352]{1,0:T(4,128)(2,1)S(1)} %get-tuple-element.56), channel_id=1, source_target_pairs={{0,12},{4,0},{8,4},{12,8},{1,13},{5,1},{9,5},{13,9},{2,14},{6,2},{... | collective-permute-start | bytes 104456 | tf_op jit(solution)/shard_map/ppermute | solution.py:34
  23.1 12.3 %collective-permute-start.6 = (bf16[128,2048]{1,0:T(8,128)(2,1)S(1)}, bf16[128,2048]{1,0:T(8,128)(2,1)S(1)}, u32[]{:S(2)}, u32[]{:S(2)}) collective-permute-start(bf16[128,2048]{1,0:T(8,128)(2,1)S(1)} %collective-permute-done.4.refs_3_), channel_id=1, source_target_pairs={{4,8},{8,4},{5,9},{9,5},{6,10},{10,6},{7,11},{11,7},{20,24},{24,20... | collective-permute-start | bytes 1572872 | tf_op jit(solution)/shard_map/ppermute | solution.py:29
  23.8 13.4 %collective-permute-start.7 = (bf16[128,2048]{1,0:T(8,128)(2,1)S(1)}, bf16[128,2048]{1,0:T(8,128)(2,1)S(1)}, u32[]{:S(2)}, u32[]{:S(2)}) collective-permute-start(bf16[128,2048]{1,0:T(8,128)(2,1)S(1)} %collective-permute-done.5.refs_1_), channel_id=1, source_target_pairs={{0,4},{4,0},{8,12},{12,8},{1,5},{5,1},{9,13},{13,9},{2,6},{6,2},{1... | collective-permute-start | bytes 1572872 | tf_op jit(solution)/shard_map/ppermute | solution.py:29
  38.1 8.3 %collective-permute-start.8 = (bf16[128,2048]{1,0:T(8,128)(2,1)S(1)}, bf16[128,2048]{1,0:T(8,128)(2,1)S(1)}, u32[]{:S(2)}, u32[]{:S(2)}) collective-permute-start(bf16[128,2048]{1,0:T(8,128)(2,1)S(1)} %choose.2.refs_0_), channel_id=1, source_target_pairs={{0,1},{1,0},{2,3},{3,2},{4,5},{5,4},{6,7},{7,6},{8,9},{9,8},{10,11... | collective-permute-start | bytes 1572872 | tf_op jit(solution)/shard_map/ppermute | solution.py:34
  38.1 14.3 %collective-permute-start.9 = (bf16[128,2048]{1,0:T(8,128)(2,1)S(1)}, bf16[128,2048]{1,0:T(8,128)(2,1)S(1)}, u32[]{:S(2)}, u32[]{:S(2)}) collective-permute-start(bf16[128,2048]{1,0:T(8,128)(2,1)S(1)} %collective-permute-done.6.refs_0_), channel_id=1, source_target_pairs={{0,4},{4,0},{8,12},{12,8},{1,5},{5,1},{9,13},{13,9},{2,6},{6,2},{1... | collective-permute-start | bytes 1572872 | tf_op jit(solution)/shard_map/ppermute | solution.py:29
  39.9 14.0 %collective-permute-start.11 = (bf16[128,2048]{1,0:T(8,128)(2,1)S(1)}, bf16[128,2048]{1,0:T(8,128)(2,1)S(1)}, u32[]{:S(2)}, u32[]{:S(2)}) collective-permute-start(bf16[128,2048]{1,0:T(8,128)(2,1)S(1)} %choose.2.refs_0_), channel_id=1, source_target_pairs={{0,2},{2,0},{1,3},{3,1},{4,6},{6,4},{5,7},{7,5},{8,10},{10,8},{9,1... | collective-permute-start | bytes 1572872 | tf_op jit(solution)/shard_map/ppermute | solution.py:34
  53.3 2.1 %collective-permute-start.13 = (bf16[128,2048]{1,0:T(8,128)(2,1)S(1)}, bf16[128,2048]{1,0:T(8,128)(2,1)S(1)}, u32[]{:S(2)}, u32[]{:S(2)}) collective-permute-start(bf16[128,2048]{1,0:T(8,128)(2,1)S(1)} %choose.3.refs_0_), channel_id=1, source_target_pairs={{0,1},{1,0},{2,3},{3,2},{4,5},{5,4},{6,7},{7,6},{8,9},{9,8},{10,11... | collective-permute-start | bytes 1572872 | tf_op jit(solution)/shard_map/ppermute | solution.py:34
  53.9 7.4 %collective-permute-start.12 = (bf16[128,2048]{1,0:T(8,128)(2,1)S(1)}, bf16[128,2048]{1,0:T(8,128)(2,1)S(1)}, u32[]{:S(2)}, u32[]{:S(2)}) collective-permute-start(bf16[128,2048]{1,0:T(8,128)(2,1)S(1)} %collective-permute-done.11.refs_0_), channel_id=1, source_target_pairs={{0,1},{1,0},{2,3},{3,2},{4,5},{5,4},{6,7},{7,6},{8,9},{9,8},{10,11... | collective-permute-start | bytes 1572872 | tf_op jit(solution)/shard_map/ppermute | solution.py:34
  53.9 14.3 %collective-permute-start.10 = (bf16[128,2048]{1,0:T(8,128)(2,1)S(1)}, bf16[128,2048]{1,0:T(8,128)(2,1)S(1)}, u32[]{:S(2)}, u32[]{:S(2)}) collective-permute-start(bf16[128,2048]{1,0:T(8,128)(2,1)S(1)} %choose.3.refs_0_), channel_id=1, source_target_pairs={{0,2},{2,0},{1,3},{3,1},{4,6},{6,4},{5,7},{7,5},{8,10},{10,8},{9,1... | collective-permute-start | bytes 1572872 | tf_op jit(solution)/shard_map/ppermute | solution.py:34
  68.3 1.9 %collective-permute-start.14 = (bf16[128,2048]{1,0:T(8,128)(2,1)S(1)}, bf16[128,2048]{1,0:T(8,128)(2,1)S(1)}, u32[]{:S(2)}, u32[]{:S(2)}) collective-permute-start(bf16[128,2048]{1,0:T(8,128)(2,1)S(1)} %collective-permute-done.10.refs_0_), channel_id=1, source_target_pairs={{0,1},{1,0},{2,3},{3,2},{4,5},{5,4},{6,7},{7,6},{8,9},{9,8},{10,11... | collective-permute-start | bytes 1572872 | tf_op jit(solution)/shard_map/ppermute | solution.py:34
where the time goes:
time: 79.5 us; the launch traced here: 79.2 us
  Pallas kernels  49.7 us (63%)
  starting transfers between devices  21.2 us (27%)
  waiting for transfers between devices  7.96 us (10%)
    pallas_call x4, Pallas kernels, correlate(): pl.pallas_call(body, grid_spec=pltpu.PrefetchScalarGridSpec(num_scalar_pr...  26.6 us
    pallas_call x4, Pallas kernels, build_hankel(): pl.pallas_call(functools.partial(hankel_kernel, v, n_win, samples, done),...  13.7 us
    ppermute x10, starting transfers between devices, turned(): lax.ppermute(block, axis, [(i, (i + distance) % size) for i in range(size)])  11.5 us
    ppermute x5, starting transfers between devices, swapped(): return lax.ppermute(block, axis, route)  9.62 us
    ppermute x10, waiting for transfers between devices, turned(): lax.ppermute(block, axis, [(i, (i + distance) % size) for i in range(size)])  5.72 us
    pallas_call x2, Pallas kernels, index(): pl.pallas_call(functools.partial(index_kernel, r_dev, lists_at, cap, tile...  5.29 us
    ppermute x5, waiting for transfers between devices, swapped(): return lax.ppermute(block, axis, route)  2.24 us
    pallas_call x2, Pallas kernels, choose(): pl.pallas_call(functools.partial(choose_kernel, which, offsets), in_specs...  1.63 us
  transfers between devices with their start and end apart: 15, of which 6 were waited for; matrix products, arithmetic and copies ran while one was open for 0% of the time, Pallas kernels for 49%

commit v1 on v0

--- a/solution.py
+++ b/solution.py
@@ -13,6 +13,7 @@
 SHIFT_ROWS = 8
 STEP = 2 * LANES
 CHAINS = 1
+COPIES = 4
 SPARE = 16
 DIGIT = 64
 HANKEL_BYTES = 24 * 2**20
@@ -113,11 +114,16 @@
 def own_kernel(source_ref, *refs):
     chain_refs, sems = refs[:-1], refs[-1]
     rows = chain_refs[0].shape[0]
+    part = rows // COPIES
     copies = []
     for chain, chain_ref in enumerate(chain_refs):
-        start = pl.multiple_of((lax.axis_index("rep") * CHAINS + chain) * rows, rows)
-        copies.append(pltpu.make_async_copy(source_ref.at[pl.ds(start, rows)], chain_ref, sems.at[chain]))
-        copies[-1].start()
+        for place in range(COPIES):
+            start = pl.multiple_of((lax.axis_index("rep") * CHAINS + chain) * rows + place * part, part)
+            target = chain_ref.at[pl.ds(place * part, part)]
+            copies.append(
+                pltpu.make_async_copy(source_ref.at[pl.ds(start, part)], target, sems.at[chain * COPIES + place])
+            )
+            copies[-1].start()
     for copy in copies:
         copy.wait()
 
@@ -130,7 +136,7 @@
         in_specs=[pl.BlockSpec(memory_space=pl.ANY)],
         out_specs=[pl.BlockSpec(memory_space=pltpu.VMEM)] * CHAINS,
         out_shape=[shape] * CHAINS,
-        scratch_shapes=[pltpu.SemaphoreType.DMA((CHAINS,))],
+        scratch_shapes=[pltpu.SemaphoreType.DMA((CHAINS * COPIES,))],
         compiler_params=params(VMEM_BYTES // 4),
         name="own_rows",
     )(in_hbm(sources))
@@ -139,18 +145,21 @@
 def choose_kernel(which, offsets, number_ref, *refs):
     out_ref, sems = refs[-2:]
     rows = out_ref.shape[0] // CHAINS
+    part = rows // COPIES
     where = number_ref[which]
     waits = []
     for chain in range(CHAINS):
-        target = out_ref.at[pl.ds(chain * rows, rows)]
-        for place, offset in enumerate(offsets):
-            copy = pltpu.make_async_copy(refs[chain * len(offsets) + place], target, sems.at[chain])
-
-            @pl.when(where == offset)
-            def _():
-                copy.start()
-
-        waits.append(copy)
+        for piece in range(COPIES):
+            target = out_ref.at[pl.ds(chain * rows + piece * part, part)]
+            for place, offset in enumerate(offsets):
+                source = refs[chain * len(offsets) + place].at[pl.ds(piece * part, part)]
+                copy = pltpu.make_async_copy(source, target, sems.at[chain * COPIES + piece])
+
+                @pl.when(where == offset)
+                def _():
+                    copy.start()
+
+            waits.append(copy)
     for copy in waits:
         copy.wait()
 
@@ -164,7 +173,7 @@
         in_specs=[pl.BlockSpec(memory_space=pltpu.SMEM)] + [any_spec] * len(pieces),
         out_specs=pl.BlockSpec(memory_space=pltpu.VMEM),
         out_shape=jax.ShapeDtypeStruct((rows * CHAINS, samples), BF16),
-        scratch_shapes=[pltpu.SemaphoreType.DMA((CHAINS,))],
+        scratch_shapes=[pltpu.SemaphoreType.DMA((CHAINS * COPIES,))],
         compiler_params=params(VMEM_BYTES // 4),
         name="choose",
     )(numbers, *pieces)

time: 79.5 us -> 80.5 us (1.013)
  Pallas kernels: 49.7 us -> 51.2 us
  waiting for transfers between devices: 7.96 us -> 7.01 us
    pallas_call x2, Pallas kernels: 1.63 us -> 3.08 us  [choose(): pl.pallas_call(functools.partial(choose_kernel, which, offsets), in_specs...]
    ppermute x10, waiting for transfers between devices: 5.72 us -> 4.77 us  [turned(): lax.ppermute(block, axis, [(i, (i + distance) % size) for i in range(size)])]
  transfers between devices with their start and end apart: 15 -> 15, of which waited for: 6 -> 5; matrix products, arithmetic and copies ran while one was open for 0% -> 0% of each run, Pallas kernels for 49% -> 50%
where the time goes in v1:
time: 80.5 us; the launch traced here: 80.3 us
  Pallas kernels  51.2 us (64%)
  starting transfers between devices  21.6 us (27%)
  waiting for transfers between devices  7.01 us (9%)
    pallas_call x4, Pallas kernels, correlate(): pl.pallas_call(body, grid_spec=pltpu.PrefetchScalarGridSpec(num_scalar_pr...  26.6 us
    pallas_call x4, Pallas kernels, build_hankel(): pl.pallas_call(functools.partial(hankel_kernel, v, n_win, samples, done),...  13.7 us
    ppermute x10, starting transfers between devices, turned(): lax.ppermute(block, axis, [(i, (i + distance) % size) for i in range(size)])  12 us
    ppermute x5, starting transfers between devices, swapped(): return lax.ppermute(block, axis, route)  9.62 us
    pallas_call x2, Pallas kernels, index(): pl.pallas_call(functools.partial(index_kernel, r_dev, lists_at, cap, tile...  5.29 us
    ppermute x10, waiting for transfers between devices, turned(): lax.ppermute(block, axis, [(i, (i + distance) % size) for i in range(size)])  4.77 us
    pallas_call x2, Pallas kernels, choose(): pl.pallas_call(functools.partial(choose_kernel, which, offsets), in_specs...  3.08 us
    ppermute x5, waiting for transfers between devices, swapped(): return lax.ppermute(block, axis, route)  2.24 us
  transfers between devices with their start and end apart: 15, of which 5 were waited for; matrix products, arithmetic and copies ran while one was open for 0% of the time, Pallas kernels for 50%

profile of v1, /device:TPU:0, one launch (start us, length us, event | category | flops | bytes accessed | tf_op | source)
XLA Modules:
  0.0 80.3 jit_solution(5780434249203529595)
XLA Ops:
  1.1 3.1 %collective-permute-start.4 = (bf16[128,2048]{1,0:T(8,128)(2,1)S(1)}, bf16[128,2048]{1,0:T(8,128)(2,1)S(1)}, u32[]{:S(2)}, u32[]{:S(2)}) collective-permute-start(bf16[128,2048]{1,0:T(8,128)(2,1)S(1)} %own_rows.1.refs_2_), channel_id=1, source_target_pairs={{0,4},{4,0},{8,12},{12,8},{1,5},{5,1},{9,13},{13,9},{2,6},{6,2},{1... | collective-permute-start | bytes 1572872 | tf_op jit(solution)/shard_map/ppermute | solution.py:30
  4.9 1.6 %collective-permute-start = (bf16[4,2048]{1,0:T(4,128)(2,1)}, bf16[4,2048]{1,0:T(4,128)(2,1)S(1)}, u32[]{:S(2)}, u32[]{:S(2)}) collective-permute-start(bf16[4,2048]{1,0:T(4,128)(2,1)} %refs_0_.1), channel_id=1, source_target_pairs={{0,2},{2,0},{1,3},{3,1},{4,6},{6,4},{5,7},{7,5},{8,10},{10,8},{9,1... | collective-permute-start | bytes 49160 | tf_op jit(solution)/shard_map/ppermute | solution.py:35
  6.5 2.5 %collective-permute-done.refs_1_ = bf16[4,2048]{1,0:T(4,128)(2,1)S(1)} collective-permute-done((bf16[4,2048]{1,0:T(4,128)(2,1)}, bf16[4,2048]{1,0:T(4,128)(2,1)S(1)}, u32[]{:S(2)}, u32[]{:S(2)}) %collective-permute-start) | collective-permute-done | bytes 16416 | tf_op jit(solution)/shard_map/ppermute | solution.py:35
  8.9 1.4 %pack.1 = (bf16[4,4352]{1,0:T(4,128)(2,1)S(1)}, bf16[4,4352]{1,0:T(4,128)(2,1)S(1)}, bf16[4,4352]{1,0:T(4,128)(2,1)S(1)}, bf16[4,4352]{1,0:T(4,128)(2,1)S(1)}, s32[7]{0:T(128)S(1)}) custom-call(s32[1,2]{1,0:T(1,128)} %plan_hbm.1, s32[4,512]{1,0:T(4,128)} %bitcast.5, s32[4,512]{1,0:T(4,128)} %bitcast.6, bf16[4,2048]{1,0:T(4,128)(2,1)} %refs_0_.1, ...), custom_call_target="tpu_custom_call" | custom-call | tf_op jit(solution)/shard_map/pack/pallas_call | solution.py:95
  10.4 4.4 %collective-permute-start.1 = (bf16[4,4352]{1,0:T(4,128)(2,1)S(1)}, bf16[4,4352]{1,0:T(4,128)(2,1)S(1)}, u32[]{:S(2)}, u32[]{:S(2)}) collective-permute-start(bf16[4,4352]{1,0:T(4,128)(2,1)S(1)} %get-tuple-element.54), channel_id=1, source_target_pairs={{0,4},{4,8},{8,12},{12,0},{1,5},{5,9},{9,13},{13,1},{2,6},{6,10},{... | collective-permute-start | bytes 104456 | tf_op jit(solution)/shard_map/ppermute | solution.py:35
  14.8 2.4 %collective-permute-start.3 = (bf16[4,4352]{1,0:T(4,128)(2,1)S(1)}, bf16[4,4352]{1,0:T(4,128)(2,1)S(1)}, u32[]{:S(2)}, u32[]{:S(2)}) collective-permute-start(bf16[4,4352]{1,0:T(4,128)(2,1)S(1)} %get-tuple-element.56), channel_id=1, source_target_pairs={{0,12},{4,0},{8,4},{12,8},{1,13},{5,1},{9,5},{13,9},{2,14},{6,2},{... | collective-permute-start | bytes 104456 | tf_op jit(solution)/shard_map/ppermute | solution.py:35
  17.2 2.0 %index.2 = (bf16[4,640,256]{2,1,0:T(8,128)(2,1)S(1)}, bf16[4,512,512]{2,1,0:T(8,128)(2,1)S(1)}, s32[4]{0:T(128)S(1)}, s32[16]{0:T(128)S(1)}, bf16[4,4,640,256]{3...) custom-call(s32[7]{0:T(128)S(1)} %get-tuple-element.53.number_ref, bf16[4,4352]{1,0:T(4,128)(2,1)S(1)} %get-tuple-element.57.refs_0_), custom_call_target="tpu_custom_call" | custom-call | tf_op jit(solution)/shard_map/index/pallas_call | solution.py:277
  19.3 1.9 %hankel.5.refs_3_ = bf16[16,128,2432]{2,1,0:T(8,128)(2,1)S(1)} custom-call(s32[7]{0:T(128)S(1)} %get-tuple-element.53.number_ref, bf16[4,4352]{1,0:T(4,128)(2,1)S(1)} %get-tuple-element.57.refs_0_), custom_call_target="tpu_custom_call" | custom-call | flops 1245184 | bytes 2490368 | tf_op jit(solution)/shard_map/hankel/pallas_call | solution.py:344
  21.2 1.9 %hankel.4.refs_3_ = bf16[16,128,2432]{2,1,0:T(8,128)(2,1)S(1)} custom-call(s32[7]{0:T(128)S(1)} %get-tuple-element.53.number_ref, bf16[4,4352]{1,0:T(4,128)(2,1)S(1)} %get-tuple-element.57.refs_0_), custom_call_target="tpu_custom_call" | custom-call | flops 1245184 | bytes 2490368 | tf_op jit(solution)/shard_map/hankel/pallas_call | solution.py:344
  23.9 3.3 %collective-permute-start.7 = (bf16[128,2048]{1,0:T(8,128)(2,1)S(1)}, bf16[128,2048]{1,0:T(8,128)(2,1)S(1)}, u32[]{:S(2)}, u32[]{:S(2)}) collective-permute-start(bf16[128,2048]{1,0:T(8,128)(2,1)S(1)} %collective-permute-done.5.refs_1_), channel_id=1, source_target_pairs={{0,4},{4,0},{8,12},{12,8},{1,5},{5,1},{9,13},{13,9},{2,6},{6,2},{1... | collective-permute-start | bytes 1572872 | tf_op jit(solution)/shard_map/ppermute | solution.py:30
  27.3 3.2 %index.3 = (bf16[4,640,256]{2,1,0:T(8,128)(2,1)S(1)}, bf16[4,512,512]{2,1,0:T(8,128)(2,1)S(1)}, s32[4]{0:T(128)S(1)}, s32[16]{0:T(128)S(1)}, bf16[4,4,640,256]{3...) custom-call(s32[7]{0:T(128)S(1)} %get-tuple-element.53.number_ref, ...), custom_call_target="tpu_custom_call", output_to_operand_aliasing={{0}: (4, {}), {1}: (5, {}), {4}: (8, {}), {5}: (9, {})} | custom-call | tf_op jit(solution)/shard_map/index/pallas_call | solution.py:277
  30.5 4.9 %hankel.6.refs_2_ = bf16[16,128,2432]{2,1,0:T(8,128)(2,1)S(1)} custom-call(s32[7]{0:T(128)S(1)} %get-tuple-element.53.number_ref, bf16[4,4352]{1,0:T(4,128)(2,1)S(1)} %collective-permute-done.1.refs_0_, bf16[4,4352]{1,0:T(4,128)(2,1)S(1)} %collective-permute-done.2.refs_1_, ...), custom_call_target="tpu_custom_call", output_to_operand_aliasing={{}: (4, {})} | custom-call | flops 3735552 | bytes 7471104 | tf_op jit(solution)/shard_map/hankel/pallas_call | solution.py:344
  35.5 1.9 %collective-permute-done.7.refs_4_ = bf16[128,2048]{1,0:T(8,128)(2,1)S(1)} collective-permute-done((bf16[128,2048]{1,0:T(8,128)(2,1)S(1)}, bf16[128,2048]{1,0:T(8,128)(2,1)S(1)}, u32[]{:S(2)}, u32[]{:S(2)}) %collective-permute-start.7) | collective-permute-done | bytes 524320 | tf_op jit(solution)/shard_map/ppermute | solution.py:30
  37.3 1.5 %choose.2.refs_0_ = bf16[128,2048]{1,0:T(8,128)(2,1)S(1)} custom-call(s32[7]{0:T(128)S(1)} %get-tuple-element.53.number_ref, bf16[128,2048]{1,0:T(8,128)(2,1)S(1)} %collective-permute-done.6.refs_0_, bf16[128,2048]{1,0:T(8,128)(2,1)S(1)} %collective-permute-done.5.refs_1_, bf16[128,2048]{1,0:T(8,128)(2,1)S(1)} %own_rows.1.refs_2_, ...), custom_call_target="tpu_custom_call" | custom-call | tf_op jit(solution)/shard_map/choose/pallas_call | solution.py:171
  38.9 1.8 %collective-permute-start.9 = (bf16[128,2048]{1,0:T(8,128)(2,1)S(1)}, bf16[128,2048]{1,0:T(8,128)(2,1)S(1)}, u32[]{:S(2)}, u32[]{:S(2)}) collective-permute-start(bf16[128,2048]{1,0:T(8,128)(2,1)S(1)} %collective-permute-done.6.refs_0_), channel_id=1, source_target_pairs={{0,4},{4,0},{8,12},{12,8},{1,5},{5,1},{9,13},{13,9},{2,6},{6,2},{1... | collective-permute-start | bytes 1572872 | tf_op jit(solution)/shard_map/ppermute | solution.py:30
  40.7 1.5 %collective-permute-start.11 = (bf16[128,2048]{1,0:T(8,128)(2,1)S(1)}, bf16[128,2048]{1,0:T(8,128)(2,1)S(1)}, u32[]{:S(2)}, u32[]{:S(2)}) collective-permute-start(bf16[128,2048]{1,0:T(8,128)(2,1)S(1)} %choose.2.refs_0_), channel_id=1, source_target_pairs={{0,2},{2,0},{1,3},{3,1},{4,6},{6,4},{5,7},{7,5},{8,10},{10,8},{9,1... | collective-permute-start | bytes 1572872 | tf_op jit(solution)/shard_map/ppermute | solution.py:35
  42.2 4.9 %hankel.7.refs_2_ = bf16[16,128,2432]{2,1,0:T(8,128)(2,1)S(1)} custom-call(s32[7]{0:T(128)S(1)} %get-tuple-element.53.number_ref, bf16[4,4352]{1,0:T(4,128)(2,1)S(1)} %collective-permute-done.1.refs_0_, bf16[4,4352]{1,0:T(4,128)(2,1)S(1)} %collective-permute-done.2.refs_1_, ...), custom_call_target="tpu_custom_call", output_to_operand_aliasing={{}: (4, {})} | custom-call | flops 3735552 | bytes 7471104 | tf_op jit(solution)/shard_map/hankel/pallas_call | solution.py:344
  47.2 5.7 %correlate.4 = (f32[4,512,512]{2,1,0:T(8,128)S(1)}, f32[4,512,512]{2,1,0:T(8,128)}) custom-call(s32[4]{0:T(128)S(1)} %get-tuple-element.72.pass_ref, s32[16]{0:T(128)S(1)} %get-tuple-element.73.count_ref, s32[7]{0:T(128)S(1)} %get-tuple-element.53.number_ref, bf16[128,2048]{1,0:T(8,128)(2,1)S(1)} %choose.2.refs_0_, ...), custom_call_target="tpu_custom_call" | custom-call | flops 4026531840 | bytes 8388608 | tf_op jit(solution)/shard_map/correlate/pallas_call | solution.py:550
  53.3 1.6 %choose.3.refs_0_ = bf16[128,2048]{1,0:T(8,128)(2,1)S(1)} custom-call(s32[7]{0:T(128)S(1)} %get-tuple-element.53.number_ref, bf16[128,2048]{1,0:T(8,128)(2,1)S(1)} %collective-permute-done.6.refs_0_, bf16[128,2048]{1,0:T(8,128)(2,1)S(1)} %collective-permute-done.5.refs_1_, bf16[128,2048]{1,0:T(8,128)(2,1)S(1)} %own_rows.1.refs_2_, ...), custom_call_target="tpu_custom_call" | custom-call | tf_op jit(solution)/shard_map/choose/pallas_call | solution.py:171
  55.4 1.5 %collective-permute-start.10 = (bf16[128,2048]{1,0:T(8,128)(2,1)S(1)}, bf16[128,2048]{1,0:T(8,128)(2,1)S(1)}, u32[]{:S(2)}, u32[]{:S(2)}) collective-permute-start(bf16[128,2048]{1,0:T(8,128)(2,1)S(1)} %choose.3.refs_0_), channel_id=1, source_target_pairs={{0,2},{2,0},{1,3},{3,1},{4,6},{6,4},{5,7},{7,5},{8,10},{10,8},{9,1... | collective-permute-start | bytes 1572872 | tf_op jit(solution)/shard_map/ppermute | solution.py:35
  56.9 5.9 %correlate.5 = (f32[4,512,512]{2,1,0:T(8,128)S(1)}, f32[4,512,512]{2,1,0:T(8,128)}) custom-call(s32[4]{0:T(128)S(1)} %get-tuple-element.72.pass_ref, s32[16]{0:T(128)S(1)} %get-tuple-element.73.count_ref, s32[7]{0:T(128)S(1)} %get-tuple-element.53.number_ref, bf16[128,2048]{1,0:T(8,128)(2,1)S(1)} %choose.3.refs_0_, ...), custom_call_target="tpu_custom_call", output_to_operand_aliasing={{0}: (10, {})} | custom-call | flops 4026531840 | bytes 8388608 | tf_op jit(solution)/shard_map/correlate/pallas_call | solution.py:550
  62.8 6.1 %correlate.6 = (f32[4,512,512]{2,1,0:T(8,128)S(1)}, f32[4,512,512]{2,1,0:T(8,128)}) custom-call(s32[4]{0:T(128)S(1)} %get-tuple-element.72.pass_ref, s32[16]{0:T(128)S(1)} %get-tuple-element.73.count_ref, s32[7]{0:T(128)S(1)} %get-tuple-element.53.number_ref, ...), custom_call_target="tpu_custom_call", output_to_operand_aliasing={{0}: (10, {})} | custom-call | flops 4026531840 | bytes 8388608 | tf_op jit(solution)/shard_map/correlate/pallas_call | solution.py:550
  69.4 1.9 %collective-permute-done.14.refs_1_ = bf16[128,2048]{1,0:T(8,128)(2,1)S(1)} collective-permute-done((bf16[128,2048]{1,0:T(8,128)(2,1)S(1)}, bf16[128,2048]{1,0:T(8,128)(2,1)S(1)}, u32[]{:S(2)}, u32[]{:S(2)}) %collective-permute-start.14) | collective-permute-done | bytes 524320 | tf_op jit(solution)/shard_map/ppermute | solution.py:35
  71.3 8.8 %correlate.7 = f32[4,512,512]{2,1,0:T(8,128)} custom-call(s32[4]{0:T(128)S(1)} %get-tuple-element.72.pass_ref, s32[16]{0:T(128)S(1)} %get-tuple-element.73.count_ref, s32[7]{0:T(128)S(1)} %get-tuple-element.53.number_ref, bf16[128,2048]{1,0:T(8,128)(2,1)S(1)} %collective-permute-done.10.refs_0_, bf16[128,2048]{1,0:T(8,128)(2,1)S(1)} %collective-permute-done.14.refs_1_, ...), custom_call_target="tpu_custom_call" | custom-call | flops 4026531840 | bytes 8388608 | tf_op jit(solution)/shard_map/correlate/pallas_call | solution.py:550
  (20 shorter events, 3.9 us)
Async XLA Ops:
  1.1 22.1 %collective-permute-start.4 = (bf16[128,2048]{1,0:T(8,128)(2,1)S(1)}, bf16[128,2048]{1,0:T(8,128)(2,1)S(1)}, u32[]{:S(2)}, u32[]{:S(2)}) collective-permute-start(bf16[128,2048]{1,0:T(8,128)(2,1)S(1)} %own_rows.1.refs_2_), channel_id=1, source_target_pairs={{0,4},{4,0},{8,12},{12,8},{1,5},{5,1},{9,13},{13,9},{2,6},{6,2},{1... | collective-permute-start | bytes 1572872 | tf_op jit(solution)/shard_map/ppermute | solution.py:30
  4.2 19.7 %collective-permute-start.5 = (bf16[128,2048]{1,0:T(8,128)(2,1)S(1)}, bf16[128,2048]{1,0:T(8,128)(2,1)S(1)}, u32[]{:S(2)}, u32[]{:S(2)}) collective-permute-start(bf16[128,2048]{1,0:T(8,128)(2,1)S(1)} %own_rows.1.refs_2_), channel_id=1, source_target_pairs={{4,8},{8,4},{5,9},{9,5},{6,10},{10,6},{7,11},{11,7},{20,24},{24,20... | collective-permute-start | bytes 1572872 | tf_op jit(solution)/shard_map/ppermute | solution.py:30
  4.9 4.0 %collective-permute-start = (bf16[4,2048]{1,0:T(4,128)(2,1)}, bf16[4,2048]{1,0:T(4,128)(2,1)S(1)}, u32[]{:S(2)}, u32[]{:S(2)}) collective-permute-start(bf16[4,2048]{1,0:T(4,128)(2,1)} %refs_0_.1), channel_id=1, source_target_pairs={{0,2},{2,0},{1,3},{3,1},{4,6},{6,4},{5,7},{7,5},{8,10},{10,8},{9,1... | collective-permute-start | bytes 49160 | tf_op jit(solution)/shard_map/ppermute | solution.py:35
  10.4 12.8 %collective-permute-start.1 = (bf16[4,4352]{1,0:T(4,128)(2,1)S(1)}, bf16[4,4352]{1,0:T(4,128)(2,1)S(1)}, u32[]{:S(2)}, u32[]{:S(2)}) collective-permute-start(bf16[4,4352]{1,0:T(4,128)(2,1)S(1)} %get-tuple-element.54), channel_id=1, source_target_pairs={{0,4},{4,8},{8,12},{12,0},{1,5},{5,9},{9,13},{13,1},{2,6},{6,10},{... | collective-permute-start | bytes 104456 | tf_op jit(solution)/shard_map/ppermute | solution.py:35
  14.8 8.4 %collective-permute-start.2 = (bf16[4,4352]{1,0:T(4,128)(2,1)S(1)}, bf16[4,4352]{1,0:T(4,128)(2,1)S(1)}, u32[]{:S(2)}, u32[]{:S(2)}) collective-permute-start(bf16[4,4352]{1,0:T(4,128)(2,1)S(1)} %get-tuple-element.55), channel_id=1, source_target_pairs={{0,8},{4,12},{8,0},{12,4},{1,9},{5,13},{9,1},{13,5},{2,10},{6,14},... | collective-permute-start | bytes 104456 | tf_op jit(solution)/shard_map/ppermute | solution.py:35
  14.8 8.4 %collective-permute-start.3 = (bf16[4,4352]{1,0:T(4,128)(2,1)S(1)}, bf16[4,4352]{1,0:T(4,128)(2,1)S(1)}, u32[]{:S(2)}, u32[]{:S(2)}) collective-permute-start(bf16[4,4352]{1,0:T(4,128)(2,1)S(1)} %get-tuple-element.56), channel_id=1, source_target_pairs={{0,12},{4,0},{8,4},{12,8},{1,13},{5,1},{9,5},{13,9},{2,14},{6,2},{... | collective-permute-start | bytes 104456 | tf_op jit(solution)/shard_map/ppermute | solution.py:35
  23.2 12.3 %collective-permute-start.6 = (bf16[128,2048]{1,0:T(8,128)(2,1)S(1)}, bf16[128,2048]{1,0:T(8,128)(2,1)S(1)}, u32[]{:S(2)}, u32[]{:S(2)}) collective-permute-start(bf16[128,2048]{1,0:T(8,128)(2,1)S(1)} %collective-permute-done.4.refs_3_), channel_id=1, source_target_pairs={{4,8},{8,4},{5,9},{9,5},{6,10},{10,6},{7,11},{11,7},{20,24},{24,20... | collective-permute-start | bytes 1572872 | tf_op jit(solution)/shard_map/ppermute | solution.py:30
  23.9 13.4 %collective-permute-start.7 = (bf16[128,2048]{1,0:T(8,128)(2,1)S(1)}, bf16[128,2048]{1,0:T(8,128)(2,1)S(1)}, u32[]{:S(2)}, u32[]{:S(2)}) collective-permute-start(bf16[128,2048]{1,0:T(8,128)(2,1)S(1)} %collective-permute-done.5.refs_1_), channel_id=1, source_target_pairs={{0,4},{4,0},{8,12},{12,8},{1,5},{5,1},{9,13},{13,9},{2,6},{6,2},{1... | collective-permute-start | bytes 1572872 | tf_op jit(solution)/shard_map/ppermute | solution.py:30
  38.9 8.3 %collective-permute-start.8 = (bf16[128,2048]{1,0:T(8,128)(2,1)S(1)}, bf16[128,2048]{1,0:T(8,128)(2,1)S(1)}, u32[]{:S(2)}, u32[]{:S(2)}) collective-permute-start(bf16[128,2048]{1,0:T(8,128)(2,1)S(1)} %choose.2.refs_0_), channel_id=1, source_target_pairs={{0,1},{1,0},{2,3},{3,2},{4,5},{5,4},{6,7},{7,6},{8,9},{9,8},{10,11... | collective-permute-start | bytes 1572872 | tf_op jit(solution)/shard_map/ppermute | solution.py:35
  38.9 14.3 %collective-permute-start.9 = (bf16[128,2048]{1,0:T(8,128)(2,1)S(1)}, bf16[128,2048]{1,0:T(8,128)(2,1)S(1)}, u32[]{:S(2)}, u32[]{:S(2)}) collective-permute-start(bf16[128,2048]{1,0:T(8,128)(2,1)S(1)} %collective-permute-done.6.refs_0_), channel_id=1, source_target_pairs={{0,4},{4,0},{8,12},{12,8},{1,5},{5,1},{9,13},{13,9},{2,6},{6,2},{1... | collective-permute-start | bytes 1572872 | tf_op jit(solution)/shard_map/ppermute | solution.py:30
  40.7 14.2 %collective-permute-start.11 = (bf16[128,2048]{1,0:T(8,128)(2,1)S(1)}, bf16[128,2048]{1,0:T(8,128)(2,1)S(1)}, u32[]{:S(2)}, u32[]{:S(2)}) collective-permute-start(bf16[128,2048]{1,0:T(8,128)(2,1)S(1)} %choose.2.refs_0_), channel_id=1, source_target_pairs={{0,2},{2,0},{1,3},{3,1},{4,6},{6,4},{5,7},{7,5},{8,10},{10,8},{9,1... | collective-permute-start | bytes 1572872 | tf_op jit(solution)/shard_map/ppermute | solution.py:35
  54.9 2.1 %collective-permute-start.13 = (bf16[128,2048]{1,0:T(8,128)(2,1)S(1)}, bf16[128,2048]{1,0:T(8,128)(2,1)S(1)}, u32[]{:S(2)}, u32[]{:S(2)}) collective-permute-start(bf16[128,2048]{1,0:T(8,128)(2,1)S(1)} %choose.3.refs_0_), channel_id=1, source_target_pairs={{0,1},{1,0},{2,3},{3,2},{4,5},{5,4},{6,7},{7,6},{8,9},{9,8},{10,11... | collective-permute-start | bytes 1572872 | tf_op jit(solution)/shard_map/ppermute | solution.py:35
  54.9 7.9 %collective-permute-start.12 = (bf16[128,2048]{1,0:T(8,128)(2,1)S(1)}, bf16[128,2048]{1,0:T(8,128)(2,1)S(1)}, u32[]{:S(2)}, u32[]{:S(2)}) collective-permute-start(bf16[128,2048]{1,0:T(8,128)(2,1)S(1)} %collective-permute-done.11.refs_0_), channel_id=1, source_target_pairs={{0,1},{1,0},{2,3},{3,2},{4,5},{5,4},{6,7},{7,6},{8,9},{9,8},{10,11... | collective-permute-start | bytes 1572872 | tf_op jit(solution)/shard_map/ppermute | solution.py:35
  55.4 13.9 %collective-permute-start.10 = (bf16[128,2048]{1,0:T(8,128)(2,1)S(1)}, bf16[128,2048]{1,0:T(8,128)(2,1)S(1)}, u32[]{:S(2)}, u32[]{:S(2)}) collective-permute-start(bf16[128,2048]{1,0:T(8,128)(2,1)S(1)} %choose.3.refs_0_), channel_id=1, source_target_pairs={{0,2},{2,0},{1,3},{3,1},{4,6},{6,4},{5,7},{7,5},{8,10},{10,8},{9,1... | collective-permute-start | bytes 1572872 | tf_op jit(solution)/shard_map/ppermute | solution.py:35
  69.4 1.9 %collective-permute-start.14 = (bf16[128,2048]{1,0:T(8,128)(2,1)S(1)}, bf16[128,2048]{1,0:T(8,128)(2,1)S(1)}, u32[]{:S(2)}, u32[]{:S(2)}) collective-permute-start(bf16[128,2048]{1,0:T(8,128)(2,1)S(1)} %collective-permute-done.10.refs_0_), channel_id=1, source_target_pairs={{0,1},{1,0},{2,3},{3,2},{4,5},{5,4},{6,7},{7,6},{8,9},{9,8},{10,11... | collective-permute-start | bytes 1572872 | tf_op jit(solution)/shard_map/ppermute | solution.py:35
